TPU v7x, 32 devices: a whole 2x2x4 slice. The times are simulated.
32 devices in a mesh: pipe: 2 (over core), dp: 8 (over z, x), tensor: 2 (over y).
Axes of the slice: x: 2, y: 2, z: 4, core: 2. Of those that a mesh axis runs over, the one named last changes fastest.
Arguments:
- block_input: bfloat16 [8, 2, 256, 768], P('dp', None, 'tensor'), may hold values from -6 to 6
- cotangent: bfloat16 [8, 2, 256, 768], P('dp', None, 'tensor'), may hold values from -6 to 6
- lengths: int32 [8, 2, 2], P('dp'), may hold values from 0 to 256, as said below
- ln1_gain: float32 [2, 768], P('pipe'), may hold values from 0.5 to 1.5
- ln1_bias: float32 [2, 768], P('pipe'), may hold values from -2.5 to 2.5
- qkv_weight: bfloat16 [2, 768, 3, 768], P('pipe', None, None, 'tensor'), may hold values from -0.21875 to 0.21875
- qv_bias: float32 [2, 2, 12, 64], P('pipe', None, 'tensor'), may hold values from -2.5 to 2.5
- proj_weight: bfloat16 [2, 768, 768], P('pipe', 'tensor'), may hold values from -0.875 to 0.875
- proj_bias: float32 [2, 768], P('pipe'), may hold values from -2.5 to 2.5
- ln2_gain: float32 [2, 768], P('pipe'), may hold values from 0.5 to 1.5
- ln2_bias: float32 [2, 768], P('pipe'), may hold values from -2.5 to 2.5
- fc_weight: bfloat16 [2, 768, 3072], P('pipe', None, 'tensor'), may hold values from -0.21875 to 0.21875
- fc_bias: float32 [2, 4, 768], P('pipe', 'tensor'), may hold values from -2.5 to 2.5
- out_weight: bfloat16 [2, 3072, 768], P('pipe', 'tensor'), may hold values from -0.15625 to 0.15625
- out_bias: float32 [2, 768], P('pipe'), may hold values from -2.5 to 2.5
Outputs:
- block_outputs: bfloat16 [2, 8, 2, 256, 768], P('pipe', 'dp', None, 'tensor')
- input_grads: bfloat16 [2, 8, 2, 256, 768], P('pipe', 'dp', None, 'tensor')
- grad_ln1_gain: float32 [2, 768], P('pipe', ('dp', 'tensor'))
- grad_ln1_bias: float32 [2, 768], P('pipe', ('dp', 'tensor'))
- grad_qkv_weight: float32 [2, 768, 3, 768], P('pipe', 'dp', None, 'tensor')
- grad_qv_bias: float32 [2, 2, 12, 64], P('pipe', None, 'tensor', 'dp')
- grad_proj_weight: float32 [2, 768, 768], P('pipe', 'tensor', 'dp')
- grad_proj_bias: float32 [2, 768], P('pipe', ('dp', 'tensor'))
- grad_ln2_gain: float32 [2, 768], P('pipe', ('dp', 'tensor'))
- grad_ln2_bias: float32 [2, 768], P('pipe', ('dp', 'tensor'))
- grad_fc_weight: float32 [2, 768, 3072], P('pipe', 'dp', 'tensor')
- grad_fc_bias: float32 [2, 4, 768], P('pipe', 'tensor', 'dp')
- grad_out_weight: float32 [2, 3072, 768], P('pipe', 'tensor', 'dp')
- grad_out_bias: float32 [2, 768], P('pipe', ('dp', 'tensor'))
Inputs may be any that keep to these rules, and one draw needn't show every extreme that they name: `lengths`: each micro-batch holds one sequence of 129 to 256 tokens in slot 0 and 0 in slot 1, or two sequences of 1 to 128 tokens; some micro-batch holds exactly 256 tokens in slot 0.
All inputs are finite; a program needn't handle non-finite values.
Results may differ from a plain program's by a relative error of at most 0.02.
Values may be sent and summed in bfloat16 or wider, within the bound.
A program may use at most 128 MiB of HBM per device.

v0:
```python
import math

import jax
import jax.numpy as jnp
from jax import lax
from jax.sharding import PartitionSpec as P

EPSILON = 1e-05
MASKED = -1000000000.0


def shifted(block, axis, distance):
    devices = range(lax.axis_size(axis))
    route = [(i - distance, i) for i in devices if i - distance in devices]
    return lax.ppermute(block, axis, route)


def normalize(values, gain_vec, shift_vec):
    row_mean = jnp.mean(values, axis=-1, keepdims=True)
    centered = values - row_mean
    inv_std = lax.rsqrt(jnp.mean(centered * centered, axis=-1, keepdims=True) + EPSILON)
    normed = centered * inv_std
    return (normed * gain_vec + shift_vec, normed, inv_std)


def normalize_back(gradient, normed, inv_std, gain_vec):
    scaled = gradient * gain_vec
    centered_grad = (
        scaled
        - jnp.mean(scaled, axis=-1, keepdims=True)
        - normed * jnp.mean(scaled * normed, axis=-1, keepdims=True)
    )
    return (inv_std * centered_grad, jnp.sum(gradient * normed, axis=0), jnp.sum(gradient, axis=0))


def gelu_tanh(values):
    return jax.nn.gelu(values, approximate=True)


def segment_ids(length_pair, all_rows, tile_rows):
    start_two = (length_pair[0] + tile_rows - 1) // tile_rows * tile_rows
    position = jnp.arange(all_rows, dtype=jnp.int32)
    inside_two = (position >= start_two) & (position < start_two + length_pair[1])
    return jnp.where(position < length_pair[0], 0, jnp.where(inside_two, 1, position + 2))


def score_mask(segment):
    position = jnp.arange(segment.shape[0], dtype=jnp.int32)
    return (segment[:, None] == segment[None, :]) & (position[None, :] <= position[:, None])


def scores_of(queries, key_rows, allowed, score_scale):
    raw_scores = (
        jnp.einsum("qhe,khe->hqk", queries, key_rows, preferred_element_type=jnp.float32)
        * score_scale
    )
    return jnp.where(allowed[None], raw_scores, MASKED)


def run_if(active, work, blank, operand):
    return lax.cond(active, work, lambda unused: blank, operand)


def take_slot(buffer, slot_index):
    return lax.dynamic_index_in_dim(buffer, slot_index, 0, keepdims=False)


def store_slot(buffer, update, slot_index, active):
    previous = take_slot(buffer, slot_index)
    return lax.dynamic_update_index_in_dim(
        buffer, jnp.where(active, update, previous), slot_index, 0
    )


def pack_blocks(grads, dims, groups):
    pieces = [
        jnp.moveaxis(grad, dim_number, 0).reshape(groups, -1)
        for grad, dim_number in zip(grads, dims)
    ]
    return jnp.concatenate(pieces, axis=1)


def unpack_blocks(summed, shapes, dims, groups):
    results = []
    start = 0
    for shape_in, dim_number in zip(shapes, dims):
        moved = (shape_in[dim_number] // groups,) + tuple(
            (extent for number, extent in enumerate(shape_in) if number != dim_number)
        )
        count = math.prod(moved)
        piece = summed[start : start + count].reshape(moved)
        results.append(jnp.moveaxis(piece, 0, dim_number))
        start = start + count
    return tuple(results)


def local(
    block_input,
    cotangent,
    lengths,
    ln1_gain,
    ln1_bias,
    qkv_weight,
    qv_bias,
    proj_weight,
    proj_bias,
    ln2_gain,
    ln2_bias,
    fc_weight,
    fc_bias,
    out_weight,
    out_bias,
):
    f32 = jnp.float32
    bf16 = jnp.bfloat16
    section_index = lax.axis_index("pipe")
    portion = lax.axis_index("tensor")
    groups = lax.axis_size("dp")
    batches = block_input.shape[1]
    half_rows = block_input.shape[2]
    features = block_input.shape[3]
    all_rows = half_rows * lax.axis_size("tensor")
    tile_rows = all_rows // 2
    heads_here = qv_bias.shape[2]
    head_size = qv_bias.shape[3]
    inner_width = heads_here * head_size
    hidden_here = fc_weight.shape[2]
    score_scale = 1.0 / math.sqrt(head_size)
    gain_one, shift_one = (ln1_gain[0], ln1_bias[0])
    gain_two, shift_two = (ln2_gain[0], ln2_bias[0])
    w_qkv = qkv_weight[0]
    w_proj = proj_weight[0]
    w_fc = fc_weight[0]
    w_out = out_weight[0]
    b_proj = proj_bias[0]
    b_out = out_bias[0]
    b_fc = fc_bias[0].reshape(hidden_here)
    b_mixed = jnp.stack(
        [
            qv_bias[0, 0].reshape(inner_width),
            jnp.zeros((inner_width,), f32),
            qv_bias[0, 1].reshape(inner_width),
        ]
    )
    own_inputs = block_input[0]
    own_grads = cotangent[0]
    segments = jax.vmap(lambda length_pair: segment_ids(length_pair, all_rows, tile_rows))(
        lengths[0]
    )
    valid_rows = (lax.dynamic_slice_in_dim(segments, portion * half_rows, half_rows, 1) < 2).astype(
        f32
    )
    head_shape = (all_rows, heads_here, head_size)

    def attention_forward(operand):
        gathered, segment = operand
        mixed = jnp.einsum("rd,dch->rch", gathered, w_qkv, preferred_element_type=f32)
        mixed = (mixed + b_mixed).astype(bf16)
        queries = mixed[:, 0].reshape(head_shape)
        key_rows = mixed[:, 1].reshape(head_shape)
        values = mixed[:, 2].reshape(head_shape)
        scores = scores_of(queries, key_rows, score_mask(segment), score_scale)
        row_top = jnp.max(scores, axis=-1, keepdims=True)
        exp_scores = jnp.exp(scores - row_top)
        row_total = jnp.sum(exp_scores, axis=-1, keepdims=True)
        probs = (exp_scores / row_total).astype(bf16)
        attended = jnp.einsum("hqk,khe->qhe", probs, values, preferred_element_type=f32)
        attended = attended.reshape(all_rows, inner_width).astype(bf16)
        log_total = (row_top + jnp.log(row_total))[:, :, 0]
        partial_value = jnp.dot(attended, w_proj, preferred_element_type=f32)
        return (partial_value, mixed, attended, log_total)

    def mlp_forward(gathered):
        pre_act = jnp.dot(gathered, w_fc, preferred_element_type=f32) + b_fc
        activated = gelu_tanh(pre_act).astype(bf16)
        return (jnp.dot(activated, w_out, preferred_element_type=f32), pre_act, activated)

    def mlp_backward(operand):
        gathered_grad, pre_act, activated, gathered_two = operand
        d_out_w = jnp.einsum("rf,rd->fd", activated, gathered_grad, preferred_element_type=f32)
        d_activated = jnp.einsum("rd,fd->rf", gathered_grad, w_out, preferred_element_type=f32)
        d_pre = jax.vjp(gelu_tanh, pre_act)[1](d_activated)[0].astype(bf16)
        d_fc_b = jnp.sum(d_pre, axis=0, dtype=f32)
        d_fc_w = jnp.einsum("rd,rf->df", gathered_two, d_pre, preferred_element_type=f32)
        d_normed = jnp.einsum("rf,df->rd", d_pre, w_fc, preferred_element_type=f32)
        return (d_normed, (d_fc_w, d_fc_b, d_out_w))

    def attention_backward(operand):
        gathered_grad, mixed, attended, log_total, gathered_one, segment = operand
        d_proj_w = jnp.einsum("rh,rd->hd", attended, gathered_grad, preferred_element_type=f32)
        d_attended = (
            jnp.einsum("rd,hd->rh", gathered_grad, w_proj, preferred_element_type=f32)
            .astype(bf16)
            .reshape(head_shape)
        )
        queries = mixed[:, 0].reshape(head_shape)
        key_rows = mixed[:, 1].reshape(head_shape)
        values = mixed[:, 2].reshape(head_shape)
        scores = scores_of(queries, key_rows, score_mask(segment), score_scale)
        probs = jnp.exp(scores - log_total[:, :, None])
        d_values = jnp.einsum(
            "hqk,qhe->khe", probs.astype(bf16), d_attended, preferred_element_type=f32
        ).astype(bf16)
        d_probs = jnp.einsum("qhe,khe->hqk", d_attended, values, preferred_element_type=f32)
        d_scores = (probs * (d_probs - jnp.sum(d_probs * probs, axis=-1, keepdims=True))).astype(
            bf16
        )
        d_queries = (
            jnp.einsum("hqk,khe->qhe", d_scores, key_rows, preferred_element_type=f32) * score_scale
        ).astype(bf16)
        d_keys = (
            jnp.einsum("hqk,qhe->khe", d_scores, queries, preferred_element_type=f32) * score_scale
        ).astype(bf16)
        d_mixed = jnp.stack(
            [
                d_queries.reshape(all_rows, inner_width),
                d_keys.reshape(all_rows, inner_width),
                d_values.reshape(all_rows, inner_width),
            ],
            axis=1,
        )
        d_qv_b = jnp.stack(
            [jnp.sum(d_queries, axis=0, dtype=f32), jnp.sum(d_values, axis=0, dtype=f32)]
        )
        d_qkv_w = jnp.einsum("rd,rch->dch", gathered_one, d_mixed, preferred_element_type=f32)
        d_normed = jnp.einsum("rch,dch->rd", d_mixed, w_qkv, preferred_element_type=f32)
        return (d_normed, (d_qkv_w, d_qv_b, d_proj_w))

    blank_attention = (
        jnp.zeros((all_rows, features), f32),
        jnp.zeros((all_rows, 3, inner_width), bf16),
        jnp.zeros((all_rows, inner_width), bf16),
        jnp.zeros((heads_here, all_rows), f32),
    )
    blank_mlp = (
        jnp.zeros((all_rows, features), f32),
        jnp.zeros((all_rows, hidden_here), f32),
        jnp.zeros((all_rows, hidden_here), bf16),
    )
    blank_mlp_back = (
        jnp.zeros((all_rows, features), f32),
        (
            jnp.zeros((features, hidden_here), f32),
            jnp.zeros((hidden_here,), f32),
            jnp.zeros((hidden_here, features), f32),
        ),
    )
    blank_attn_back = (
        jnp.zeros((all_rows, features), f32),
        (
            jnp.zeros((features, 3, inner_width), f32),
            jnp.zeros((2, heads_here, head_size), f32),
            jnp.zeros((inner_width, features), f32),
        ),
    )

    def forward_tick(carried, step_index):
        incoming, stored, produced = carried
        batch_index = step_index - section_index
        active = (batch_index >= 0) & (batch_index < batches)
        slot_index = jnp.clip(batch_index, 0, batches - 1)
        section_rows = jnp.where(section_index == 0, take_slot(own_inputs, slot_index), incoming)
        segment = take_slot(segments, slot_index)
        valid = take_slot(valid_rows, slot_index)[:, None]
        residual = section_rows.astype(f32)
        normed_one = normalize(residual, gain_one, shift_one)[0].astype(bf16)
        gathered_one = lax.all_gather(normed_one, "tensor", axis=0, tiled=True)
        partial_value, mixed, attended, log_total = run_if(
            active, attention_forward, blank_attention, (gathered_one, segment)
        )
        after_attn = (
            residual
            + lax.psum_scatter(
                partial_value.astype(jnp.bfloat16), "tensor", scatter_dimension=0, tiled=True
            ).astype(jnp.float32)
            + b_proj
        )
        normed_two = normalize(after_attn, gain_two, shift_two)[0].astype(bf16)
        gathered_two = lax.all_gather(normed_two, "tensor", axis=0, tiled=True)
        partial_two, pre_act, activated = run_if(active, mlp_forward, blank_mlp, gathered_two)
        after_mlp = (
            after_attn
            + lax.psum_scatter(
                partial_two.astype(jnp.bfloat16), "tensor", scatter_dimension=0, tiled=True
            ).astype(jnp.float32)
            + b_out
        )
        result = (valid * after_mlp).astype(bf16)
        updates = (
            section_rows,
            gathered_one,
            mixed,
            log_total,
            attended,
            after_attn,
            gathered_two,
            pre_act,
            activated,
        )
        stored = tuple(
            (
                store_slot(buffer, update, slot_index, active)
                for buffer, update in zip(stored, updates)
            )
        )
        produced = store_slot(produced, result, slot_index, active)
        passed = shifted(result, "pipe", 1)
        return ((passed, stored, produced), None)

    stored_zero = (
        jnp.zeros((batches, half_rows, features), bf16),
        jnp.zeros((batches, all_rows, features), bf16),
        jnp.zeros((batches, all_rows, 3, inner_width), bf16),
        jnp.zeros((batches, heads_here, all_rows), f32),
        jnp.zeros((batches, all_rows, inner_width), bf16),
        jnp.zeros((batches, half_rows, features), f32),
        jnp.zeros((batches, all_rows, features), bf16),
        jnp.zeros((batches, all_rows, hidden_here), f32),
        jnp.zeros((batches, all_rows, hidden_here), bf16),
    )
    initial = (
        jnp.zeros((half_rows, features), bf16),
        stored_zero,
        jnp.zeros((batches, half_rows, features), bf16),
    )
    (unused_rows, stored, produced), unused_out = lax.scan(
        forward_tick, initial, jnp.arange(batches + 1)
    )
    full_shapes = (
        (features, 3, inner_width),
        (2, heads_here, head_size),
        (inner_width, features),
        (features, hidden_here),
        tuple(fc_bias.shape[1:]),
        (hidden_here, features),
    )
    split_dims = (0, 2, 1, 0, 1, 1)
    pending_zero = ()
    totals_zero = tuple((jnp.zeros(shape_in, f32) for shape_in in full_shapes))
    vectors_zero = tuple((jnp.zeros((features,), f32) for number in range(6)))

    def backward_step(carried, step_index):
        incoming, totals, pending, vectors, handed = carried
        batch_index = step_index - (1 - section_index)
        active = (batch_index >= 0) & (batch_index < batches)
        slot_index = jnp.clip(batch_index, 0, batches - 1)
        grad_rows = jnp.where(
            section_index == 1, take_slot(own_grads, slot_index), incoming
        ).astype(f32)
        (
            section_rows,
            gathered_one,
            mixed,
            log_total,
            attended,
            after_attn,
            gathered_two,
            pre_act,
            activated,
        ) = tuple((take_slot(buffer, slot_index) for buffer in stored))
        segment = take_slot(segments, slot_index)
        valid = take_slot(valid_rows, slot_index)[:, None]
        grad_mlp = valid * grad_rows
        gathered_grad = lax.all_gather(grad_mlp.astype(bf16), "tensor", axis=0, tiled=True)
        partial_value, mlp_grads = run_if(
            active, mlp_backward, blank_mlp_back, (gathered_grad, pre_act, activated, gathered_two)
        )
        d_normed_two = lax.psum_scatter(
            partial_value.astype(jnp.bfloat16), "tensor", scatter_dimension=0, tiled=True
        ).astype(jnp.float32)
        unused_two, normed_two, inv_two = normalize(after_attn, gain_two, shift_two)
        d_ln_two, d_gain_two, d_shift_two = normalize_back(
            d_normed_two, normed_two, inv_two, gain_two
        )
        grad_attn = grad_mlp + d_ln_two
        gathered_attn = lax.all_gather(grad_attn.astype(bf16), "tensor", axis=0, tiled=True)
        partial_one, attn_grads = run_if(
            active,
            attention_backward,
            blank_attn_back,
            (gathered_attn, mixed, attended, log_total, gathered_one, segment),
        )
        d_normed_one = lax.psum_scatter(
            partial_one.astype(jnp.bfloat16), "tensor", scatter_dimension=0, tiled=True
        ).astype(jnp.float32)
        unused_one, normed_one, inv_one = normalize(section_rows.astype(f32), gain_one, shift_one)
        d_ln_one, d_gain_one, d_shift_one = normalize_back(
            d_normed_one, normed_one, inv_one, gain_one
        )
        input_grad = (grad_attn + d_ln_one).astype(bf16)
        tick_vectors = (
            d_gain_one,
            d_shift_one,
            jnp.sum(grad_attn, axis=0),
            d_gain_two,
            d_shift_two,
            jnp.sum(grad_mlp, axis=0),
        )
        vectors = tuple(
            (total + jnp.where(active, term, 0.0) for total, term in zip(vectors, tick_vectors))
        )
        d_qkv_w, d_qv_b, d_proj_w = attn_grads
        d_fc_w, d_fc_b, d_out_w = mlp_grads
        tick_grads = (d_qkv_w, d_qv_b, d_proj_w, d_fc_w, d_fc_b.reshape(full_shapes[4]), d_out_w)
        totals = tuple((total + term for total, term in zip(totals, tick_grads)))
        handed = store_slot(handed, input_grad, slot_index, active)
        passed = shifted(input_grad, "pipe", -1)
        return ((passed, totals, pending, vectors, handed), None)

    initial_back = (
        jnp.zeros((half_rows, features), bf16),
        totals_zero,
        pending_zero,
        vectors_zero,
        jnp.zeros((batches, half_rows, features), bf16),
    )
    first_back, unused_first = backward_step(initial_back, jnp.int32(0))
    (unused_back, totals, unused_pending, vectors, handed), unused_steps = lax.scan(
        lambda carried, step_index: backward_step(carried, step_index),
        first_back,
        jnp.arange(1, batches + 1),
    )
    received_all = lax.all_to_all(
        pack_blocks(totals, split_dims, groups).astype(jnp.bfloat16),
        "dp",
        split_axis=0,
        concat_axis=0,
        tiled=True,
    ).astype(jnp.float32)
    totals = unpack_blocks(jnp.sum(received_all, axis=0), full_shapes, split_dims, groups)
    vectors = lax.psum_scatter(vectors, ("dp", "tensor"), scatter_dimension=0, tiled=True)
    g_qkv_w, g_qv_b, g_proj_w, g_fc_w, g_fc_b, g_out_w = totals
    g_gain_one, g_shift_one, g_proj_b, g_gain_two, g_shift_two, g_out_b = vectors
    return (
        produced[None, None],
        handed[None, None],
        g_gain_one[None],
        g_shift_one[None],
        g_qkv_w[None],
        g_qv_b[None],
        g_proj_w[None],
        g_proj_b[None],
        g_gain_two[None],
        g_shift_two[None],
        g_fc_w[None],
        g_fc_b[None],
        g_out_w[None],
        g_out_b[None],
    )


def solution(mesh):
    return jax.shard_map(
        local,
        mesh=mesh,
        in_specs=(
            P("dp", None, "tensor", None),
            P("dp", None, "tensor", None),
            P("dp", None, None),
            P("pipe", None),
            P("pipe", None),
            P("pipe", None, None, "tensor"),
            P("pipe", None, "tensor", None),
            P("pipe", "tensor", None),
            P("pipe", None),
            P("pipe", None),
            P("pipe", None),
            P("pipe", None, "tensor"),
            P("pipe", "tensor", None),
            P("pipe", "tensor", None),
            P("pipe", None),
        ),
        out_specs=(
            P("pipe", "dp", None, "tensor", None),
            P("pipe", "dp", None, "tensor", None),
            P("pipe", ("dp", "tensor")),
            P("pipe", ("dp", "tensor")),
            P("pipe", "dp", None, "tensor"),
            P("pipe", None, "tensor", "dp"),
            P("pipe", "tensor", "dp"),
            P("pipe", ("dp", "tensor")),
            P("pipe", ("dp", "tensor")),
            P("pipe", ("dp", "tensor")),
            P("pipe", "dp", "tensor"),
            P("pipe", "tensor", "dp"),
            P("pipe", "tensor", "dp"),
            P("pipe", ("dp", "tensor")),
        ),
        check_vma=False,
    )
```

profile of v0, /device:TPU:0, one launch (start us, length us, event | category | flops | bytes accessed | tf_op | source)
XLA Modules:
  0.0 923.3 jit_solution(2702232702314073714)
XLA Ops:
  14.1 8.6 all_gather.24
  33.3 238.9 %while.71 = (s32[]{:T(128)}, bf16[128,768]{1,0:T(8,128)(2,1)}, bf16[2,128,768]{2,1,0:T(8,128)(2,1)S(1)}, bf16[2,256,768]{2,1,0:T(8,128)(2,1)}, bf16[2,256,3,384]...) while((s32[]{:T(128)}, bf16[128,768]{1,0:T(8,128)(2,1)}, ...), condition=%wide.region_13.14_spmd.clone, body=%wide.region_0.13_spmd.clone.sunk | while | flops 1927055104 | bytes 104950616 | solution.py:326
  45.4 11.8 %conditional.16 = (bf16[256,768]{1,0:T(8,128)(2,1)S(1)}, bf16[256,3,384]{2,0,1:T(8,128)(2,1)S(1)}, bf16[256,384]{0,1:T(8,128)(2,1)}, f32[6,256]{1,0:T(8,128)S(1)}) conditional(s32[]{:T(128)} %convert_element_type.579, () %tuple.214, (bf16[256,768]{1,0:T(8,128)(2,1)}, bf16[768,3,384]{2,0,1:T(8,128)(2,1)S(1)}, f32[3,384]{1,0:T(4,128)}, ...), branch_computations={%region_3.3_spmd, %region_4.6_spmd} | conditional | flops 708673536 | bytes 16706196 | solution.py:61
  99.9 9.0 reduce-scatter.13.cloned.1.call-done
  119.0 7.7 all_gather.34
  126.6 11.8 %conditional.16 = (bf16[256,768]{1,0:T(8,128)(2,1)S(1)}, bf16[256,3,384]{2,0,1:T(8,128)(2,1)S(1)}, bf16[256,384]{0,1:T(8,128)(2,1)}, f32[6,256]{1,0:T(8,128)S(1)}) conditional(s32[]{:T(128)} %convert_element_type.579, () %tuple.214, (bf16[256,768]{1,0:T(8,128)(2,1)}, bf16[768,3,384]{2,0,1:T(8,128)(2,1)S(1)}, f32[3,384]{1,0:T(4,128)}, ...), branch_computations={%region_3.3_spmd, %region_4.6_spmd} | conditional | flops 708673536 | bytes 16706196 | solution.py:61
  181.5 7.9 reduce-scatter.13.cloned.1.call-done
  199.5 7.6 all_gather.34
  248.0 19.1 %reduce-scatter.13.cloned.1.call-done = bf16[128,768]{1,0:T(8,128)(2,1)} async-done(((bf16[256,768]{1,0:T(8,128)(2,1)}), bf16[128,768]{1,0:T(8,128)(2,1)}) %reduce-scatter.13.cloned.1.call-update) | async-done | bytes 196624 | tf_op jit(solution)/shard_map/while/body/eval_jaxpr/reduce_scatter | solution.py:283
  279.5 19.7 %reduce-scatter.7.cloned.1.call-done = bf16[128,768]{1,0:T(8,128)(2,1)} async-done(((bf16[256,768]{1,0:T(8,128)(2,1)}), bf16[128,768]{1,0:T(8,128)(2,1)}) %reduce-scatter.7.cloned.1.call-update) | async-done | bytes 196624 | tf_op jit(solution)/shard_map/reduce_scatter | solution.py:368
  322.7 33.2 %reduce-scatter.9.cloned.1.call-done = bf16[128,768]{1,0:T(8,128)(2,1)} async-done(((bf16[256,768]{1,0:T(8,128)(2,1)}), bf16[128,768]{1,0:T(8,128)(2,1)}) %reduce-scatter.9.cloned.1.call-update) | async-done | bytes 196624 | tf_op jit(solution)/shard_map/reduce_scatter | solution.py:383
  361.6 189.2 %while.72 = (s32[]{:T(128)}, bf16[128,768]{1,0:T(8,128)(2,1)S(1)}, f32[768,3,384]{2,0,1:T(8,128)}, f32[2,6,64]{2,1,0:T(8,128)}, f32[384,768]{1,0:T(8,128)}, /*in...) while((s32[]{:T(128)}, bf16[128,768]{1,0:T(8,128)(2,1)S(1)}, ...), condition=%wide.region_63.64_spmd.clone, body=%wide.region_38.63_spmd.clone.sunk | while | flops 3901002752 | bytes 143213264 | solution.py:418
  364.7 7.6 all_gather.36
  372.4 13.4 %conditional.18 = (bf16[256,768]{1,0:T(8,128)(2,1)S(1)}, f32[768,1536]{1,0:T(8,128)}, f32[1536,768]{1,0:T(8,128)}, f32[2,768]{1,0:T(2,128)S(1)}) conditional(s32[]{:T(128)} %convert_element_type.588, () %tuple.226, (bf16[256,768]{1,0:T(8,128)(2,1)S(1)}, bf16[1536,768]{1,0:T(8,128)(2,1)}, f32[2,256,1536]{2,1,0:T(8,128)}, s32[]{:T(128)}, ...), branch_computations={%region_41.41_spmd, %region_42.43_spmd} | conditional | flops 2424568320 | bytes 33048704 | solution.py:61
  412.3 25.0 %conditional.19 = (bf16[256,768]{1,0:T(8,128)(2,1)}, f32[768,3,384]{2,0,1:T(8,128)}, f32[2,6,64]{2,1,0:T(8,128)S(1)}, f32[384,768]{1,0:T(8,128)S(1)}) conditional(s32[]{:T(128)} %convert_element_type.588, () %tuple.228, (s32[2,256]{1,0:T(2,128)S(1)}, s32[]{:T(128)}, bf16[2,256,3,384]{1,3,2,0:T(8,128)(2,1)}, f32[2,6,256]{2,1,0:T(8,128)}, ...), branch_computations={%region_49.49_spmd, %region_50.53_spmd} | conditional | flops 1466695680 | bytes 36253060 | solution.py:61
  466.9 13.4 %conditional.18 = (bf16[256,768]{1,0:T(8,128)(2,1)S(1)}, f32[768,1536]{1,0:T(8,128)}, f32[1536,768]{1,0:T(8,128)}, f32[2,768]{1,0:T(2,128)S(1)}) conditional(s32[]{:T(128)} %convert_element_type.588, () %tuple.226, (bf16[256,768]{1,0:T(8,128)(2,1)S(1)}, bf16[1536,768]{1,0:T(8,128)(2,1)}, f32[2,256,1536]{2,1,0:T(8,128)}, s32[]{:T(128)}, ...), branch_computations={%region_41.41_spmd, %region_42.43_spmd} | conditional | flops 2424568320 | bytes 33048704 | solution.py:61
  506.4 25.0 %conditional.19 = (bf16[256,768]{1,0:T(8,128)(2,1)}, f32[768,3,384]{2,0,1:T(8,128)}, f32[2,6,64]{2,1,0:T(8,128)S(1)}, f32[384,768]{1,0:T(8,128)S(1)}) conditional(s32[]{:T(128)} %convert_element_type.588, () %tuple.228, (s32[2,256]{1,0:T(2,128)S(1)}, s32[]{:T(128)}, bf16[2,256,3,384]{1,3,2,0:T(8,128)(2,1)}, f32[2,6,256]{2,1,0:T(8,128)}, ...), branch_computations={%region_49.49_spmd, %region_50.53_spmd} | conditional | flops 1466695680 | bytes 36253060 | solution.py:61
  582.1 13.7 %dynamic-update-slice.3 = bf16[8,1,442656]{2,0,1:T(8,128)(2,1)} dynamic-update-slice(bf16[8,1,442656]{2,0,1:T(8,128)(2,1)} %dynamic-update-slice.2, bf16[8,1,147456]{2,0,1:T(8,128)(2,1)} %concatenate.26, s32[]{} %constant.525, s32[]{} %constant.525, s32[]{} %constant.528) | dynamic-update-slice | bytes 4718596
  597.2 12.7 %dynamic-update-slice.5 = bf16[8,1,442656]{2,0,1:T(8,128)(2,1)} dynamic-update-slice(bf16[8,1,442656]{2,0,1:T(8,128)(2,1)} %dynamic-update-slice.4, bf16[8,1,147456]{2,0,1:T(8,128)(2,1)S(1)} %concatenate.28, s32[]{} %constant.525, s32[]{} %constant.525, s32[]{} %constant.530) | dynamic-update-slice | bytes 4718596 | tf_op jit(solution)/shard_map/concatenate | solution.py:80
  610.5 19.5 %reduce.25 = bf16[8,442656]{1,0:T(8,128)(2,1)} reduce(bf16[8,1,442656]{2,0,1:T(8,128)(2,1)} %dynamic-update-slice.5, bf16[]{:T(256)} %broadcast.559), dimensions={1}, to_apply=%copy.117.reduce_sub_computation | reduce | bytes 14164994 | tf_op jit(solution)/shard_map/concatenate | solution.py:80
  630.0 12.3 %reshape.530 = bf16[8,2,221328]{2,1,0:T(2,128)(2,1)} reshape(bf16[8,442656]{1,0:T(8,128)(2,1)} %reduce.25) | data formatting | bytes 14164992
  649.1 209.0 %all-reduce.6 = (f32[768]{0:T(1024)S(1)}, f32[768]{0:T(1024)S(1)}, f32[768]{0:T(1024)S(1)}, f32[768]{0:T(1024)S(1)}, f32[768]{0:T(1024)S(1)}, /*index=5*/f32[768]{0:T(1024)S(1)}) all-reduce(f32[768]{0:T(1024)S(1)} %copy-done.84, f32[768]{0:T(1024)S(1)} %copy-done.81, ...), channel_id=8, replica_groups=mesh['pipe'=2,'dp'=8,'tensor'=2] {'dp','tensor'}, use_global_device_ids=true, to_apply=%region_64.65.clone | all-reduce | flops 4608 | bytes 36864
  861.6 26.4 %reshape.531 = bf16[8,1,442656]{2,1,0:T(2,128)(2,1)} reshape(bf16[8,2,221328]{2,1,0:T(2,128)(2,1)} %all-to-all-done) | data formatting | bytes 14164992
  888.0 20.1 %convert_reduce_fusion.10 = f32[442656]{0:T(1024)S(1)} fusion(bf16[8,1,442656]{2,1,0:T(2,128)(2,1)} %reshape.531), kind=kLoop, calls=%fused_computation.241 | loop fusion | flops 6639840 | bytes 8853120 | tf_op jit(solution)/shard_map/reduce_sum | solution.py:430
  (767 shorter events, 493.8 us)
Async XLA Ops:
  33.3 43.6 %reduce-scatter.11.cloned.1.call-start = ((), (), s32[]{:S(2)}) async-start(), calls=%async_computation.9 | async-start | bytes 589824 | tf_op jit(solution)/shard_map/while/body/eval_jaxpr/reduce_scatter | solution.py:273
  57.9 51.0 %reduce-scatter.13.cloned.1.call-start = ((), (), s32[]{:S(2)}) async-start(), calls=%async_computation.10 | async-start | bytes 589824 | tf_op jit(solution)/shard_map/while/body/eval_jaxpr/reduce_scatter | solution.py:283
  110.6 3.2 collective-permute-start
  113.9 44.2 %reduce-scatter.11.cloned.1.call-start = ((), (), s32[]{:S(2)}) async-start(), calls=%async_computation.9 | async-start | bytes 589824 | tf_op jit(solution)/shard_map/while/body/eval_jaxpr/reduce_scatter | solution.py:273
  139.2 50.1 %reduce-scatter.13.cloned.1.call-start = ((), (), s32[]{:S(2)}) async-start(), calls=%async_computation.10 | async-start | bytes 589824 | tf_op jit(solution)/shard_map/while/body/eval_jaxpr/reduce_scatter | solution.py:283
  191.1 3.2 collective-permute-start
  194.4 37.4 %reduce-scatter.11.cloned.1.call-start = ((), (), s32[]{:S(2)}) async-start(), calls=%async_computation.9 | async-start | bytes 589824 | tf_op jit(solution)/shard_map/while/body/eval_jaxpr/reduce_scatter | solution.py:273
  208.7 58.4 %reduce-scatter.13.cloned.1.call-start = ((), (), s32[]{:S(2)}) async-start(), calls=%async_computation.10 | async-start | bytes 589824 | tf_op jit(solution)/shard_map/while/body/eval_jaxpr/reduce_scatter | solution.py:283
  268.9 3.3 collective-permute-start
  272.2 27.0 %reduce-scatter.7.cloned.1.call-start = ((), (), s32[]{:S(2)}) async-start(), calls=%async_computation.7 | async-start | bytes 589824 | tf_op jit(solution)/shard_map/reduce_scatter | solution.py:368
  278.4 77.4 %reduce-scatter.9.cloned.1.call-start = ((), (), s32[]{:S(2)}) async-start(), calls=%async_computation.8 | async-start | bytes 589824 | tf_op jit(solution)/shard_map/reduce_scatter | solution.py:383
  318.5 37.4 %copy-start.99 = (f32[128]{0:T(128)S(1)}, f32[128]{0:T(128)}, u32[]{:S(2)}) copy-start(f32[128]{0:T(128)} %broadcast_multiply_fusion.10) | copy-start | bytes 1540
  318.5 38.6 %copy-start.45 = (f32[128,768]{1,0:T(8,128)S(1)}, f32[128,768]{1,0:T(8,128)}, u32[]{:S(2)}) copy-start(f32[128,768]{1,0:T(8,128)} %copy-done.44) | copy-start | bytes 1179652
  320.9 40.6 %copy-start.65 = (f32[2,768]{1,0:T(2,128)S(1)}, f32[2,768]{1,0:T(2,128)}, u32[]{:S(2)}) copy-start(f32[2,768]{1,0:T(2,128)} %copy-done.64) | copy-start | bytes 18436
  358.3 3.3 collective-permute-start.2
  361.8 50.4 %copy-start.9 = (bf16[384,768]{1,0:T(8,128)(2,1)}, bf16[384,768]{1,0:T(8,128)(2,1)S(1)}, u32[]{:S(2)}) copy-start(bf16[384,768]{1,0:T(8,128)(2,1)S(1)} %get-tuple-element.2522) | copy-start | bytes 1769476 | tf_op jit(solution)/shard_map/while
  361.8 40.1 %reduce-scatter.15.cloned.1.call-start = ((), (), s32[]{:S(2)}) async-start(), calls=%async_computation.11 | async-start | bytes 589824 | tf_op jit(solution)/shard_map/while/body/eval_jaxpr/reduce_scatter | solution.py:368
  386.5 64.0 %reduce-scatter.17.cloned.1.call-start = ((), (), s32[]{:S(2)}) async-start(), calls=%async_computation.12 | async-start | bytes 589824 | tf_op jit(solution)/shard_map/while/body/eval_jaxpr/reduce_scatter | solution.py:383
  452.9 3.3 collective-permute-start.1
  456.4 50.0 %copy-start.9 = (bf16[384,768]{1,0:T(8,128)(2,1)}, bf16[384,768]{1,0:T(8,128)(2,1)S(1)}, u32[]{:S(2)}) copy-start(bf16[384,768]{1,0:T(8,128)(2,1)S(1)} %get-tuple-element.2522) | copy-start | bytes 1769476 | tf_op jit(solution)/shard_map/while
  456.4 40.1 %reduce-scatter.15.cloned.1.call-start = ((), (), s32[]{:S(2)}) async-start(), calls=%async_computation.11 | async-start | bytes 589824 | tf_op jit(solution)/shard_map/while/body/eval_jaxpr/reduce_scatter | solution.py:368
  481.0 63.6 %reduce-scatter.17.cloned.1.call-start = ((), (), s32[]{:S(2)}) async-start(), calls=%async_computation.12 | async-start | bytes 589824 | tf_op jit(solution)/shard_map/while/body/eval_jaxpr/reduce_scatter | solution.py:383
  547.0 3.3 collective-permute-start.1
  642.3 219.3 %all-to-all-start = ((bf16[8,2,221328]{2,1,0:T(2,128)(2,1)}), bf16[8,2,221328]{2,1,0:T(2,128)(2,1)}, u32[]{:S(2)}, u32[]{:S(2)}) async-start(bf16[8,2,221328]{2,1,0:T(2,128)(2,1)} %reshape.530), calls=%async_computation.6 | async-start | bytes 14172160 | tf_op jit(solution)/shard_map/all_to_all | solution.py:423
  (159 other events, 1061.8 us)
Sparse Core Ops, SparseCore 0:
  58.0 14.2 reduce-scatter.10
  94.5 14.3 reduce-scatter.12
  139.3 13.1 reduce-scatter.10
  176.2 13.1 reduce-scatter.12
  208.8 22.9 reduce-scatter.10
  244.8 22.2 reduce-scatter.12
  386.6 13.1 reduce-scatter.14
  437.4 13.1 reduce-scatter.16
  481.1 13.1 reduce-scatter.14
  531.5 13.1 reduce-scatter.16
Sparse Core Ops, SparseCore 1:
  278.5 20.6 reduce-scatter.6
  314.9 40.9 reduce-scatter.8
where the time goes:
time: 935 us; the launch traced here: 923 us
  blocking collectives  295 us (32%)
  local copies, waits for them, and re-layouts  214 us (23%)
  other arithmetic  201 us (21%)
  waiting for transfers between devices  103 us (11%)
  matrix products  69.4 us (7%)
  starting transfers between devices  17.1 us (2%)
  between operations  16.8 us (2%)
    unnamed x1, blocking collectives  209 us
    unnamed x65, local copies, waits for them, and re-layouts  69.7 us
    dynamic_slice x41, local copies, waits for them, and re-layouts, take_slot(): return lax.dynamic_index_in_dim(buffer, slot_index, 0, keepdims=False)  46.5 us
    add x12, other arithmetic, backward_step(): totals = tuple((total + term for total, term in zip(totals, tick_grads)))  45 us
    dynamic_update_slice x33, other arithmetic, store_slot(): lax.dynamic_update_index_in_dim(buffer, jnp.where(active, update, previou...  43.3 us
    reduce_scatter x3, waiting for transfers between devices, backward_step(): lax.psum_scatter(partial_one.astype(jnp.bfloat16), 'tensor', scatter_dime...  36.7 us
    reduce_scatter x3, waiting for transfers between devices, forward_tick(): lax.psum_scatter(partial_two.astype(jnp.bfloat16), 'tensor', scatter_dime...  36 us
    all_gather x3, blocking collectives, backward_step(): lax.all_gather(grad_mlp.astype(bf16), 'tensor', axis=0, tiled=True)  23.9 us
  transfers between devices with their start and end apart: 19, of which 11 were waited for; matrix products, arithmetic and copies ran while one was open for 15% of the time, Pallas kernels for 0%

commit v1 on v0

v1 whole, which is shorter than its diff:
```python
import functools
import math

import jax
import jax.numpy as jnp
from jax import lax
from jax.experimental import pallas as pl
from jax.experimental.pallas import tpu as pltpu
from jax.sharding import PartitionSpec as P

EPSILON = 1e-05
MASKED = -1000000000.0
MESH = pl.DeviceIdType.MESH
F32 = jnp.float32
BF16 = jnp.bfloat16
CHUNKS = 3
GELU_A = math.sqrt(2.0 / math.pi)
GELU_B = 0.044715


def dot(a, b, ca, cb):
    return lax.dot_general(a, b, (((ca,), (cb,)), ((), ())), preferred_element_type=F32)


def norm_parts(values):
    row_mean = jnp.mean(values, axis=-1, keepdims=True)
    centered = values - row_mean
    inv_std = lax.rsqrt(jnp.mean(centered * centered, axis=-1, keepdims=True) + EPSILON)
    return centered * inv_std, inv_std


def norm_back(gradient, normed, inv_std, gain):
    scaled = gradient * gain
    return inv_std * (
        scaled
        - jnp.mean(scaled, axis=-1, keepdims=True)
        - normed * jnp.mean(scaled * normed, axis=-1, keepdims=True)
    )


def row_sum(values):
    return jnp.sum(values, axis=0, keepdims=True)


def sections_kernel(
    heads, head_size,
    x_ref, g_ref, segc_ref, segr_ref, g1_ref, s1_ref, wqkv_ref, bmix_ref, wproj_ref, bproj_ref,
    g2_ref, s2_ref, wfc_ref, bfc_ref, wout_ref, bout_ref,
    prod_ref, hand_ref, grad_ref, vec_ref,
    xin, gin, outb, inb, n1, mix, probs, att, aft, n2, act, dgl, dyb, dpre, dab, dmix, dat,
    snd, rcv, send_sem, recv_sem, first_send, first_recv, pipe_send, pipe_recv,
):
    section = lax.axis_index("pipe")
    portion = lax.axis_index("tensor")
    batches, all_rows, features = n1.shape
    inner = heads * head_size
    hidden = wfc_ref.shape[1]
    scale = 1.0 / math.sqrt(head_size)
    width = features // CHUNKS
    hwidth = hidden // CHUNKS

    barrier = pltpu.get_barrier_semaphore()
    pl.semaphore_signal(barrier, inc=1, device_id={"tensor": 1 - portion}, device_id_type=MESH)
    pl.semaphore_signal(barrier, inc=1, device_id={"pipe": 1 - section}, device_id_type=MESH)
    pl.semaphore_wait(barrier, 2)

    def first_copy(source, target):
        return pltpu.make_async_remote_copy(
            src_ref=source,
            dst_ref=target.at[:, portion],
            send_sem=first_send,
            recv_sem=first_recv,
            device_id={"tensor": 1 - portion},
            device_id_type=MESH,
        )

    def pipe_copy(source, target, m, which):
        return pltpu.make_async_remote_copy(
            src_ref=source.at[m],
            dst_ref=target.at[m],
            send_sem=pipe_send.at[m],
            recv_sem=pipe_recv.at[m],
            device_id={"pipe": 1 - section},
            device_id_type=MESH,
        )

    def swap(m, e, c):
        return pltpu.make_async_remote_copy(
            src_ref=snd.at[m, e, c],
            dst_ref=rcv.at[m, e, c],
            send_sem=send_sem.at[m, e, c],
            recv_sem=recv_sem.at[m, e, c],
            device_id={"tensor": 1 - portion},
            device_id_type=MESH,
        )

    def send_part(m, e, c, values):
        snd[m, e, c] = values.astype(BF16)
        swap(m, e, c).start()

    def total_of(m, e):
        pieces = []
        for c in range(CHUNKS):
            swap(m, e, c).wait()
            pieces.append(snd[m, e, c].astype(F32) + rcv[m, e, c].astype(F32))
        return jnp.concatenate(pieces, axis=1)

    @pl.when(section == 0)
    def _():
        first_copy(x_ref, xin).start()
        xin[:, portion] = x_ref[...]

    @pl.when(section == 1)
    def _():
        first_copy(g_ref, gin).start()
        gin[:, portion] = g_ref[...]

    vec_ref[...] = jnp.zeros_like(vec_ref)

    @pl.when(section == 0)
    def _():
        first_copy(x_ref, xin).wait()

    @pl.when(section == 1)
    def _():
        first_copy(g_ref, gin).wait()

    def forward(m, carry):
        @pl.when(section == 1)
        def _():
            pipe_copy(outb, xin, m, 0).wait_recv()

        rows = xin[m].reshape(all_rows, features).astype(F32)
        segc = segc_ref[m]
        segr = segr_ref[m]
        normed, unused = norm_parts(rows)
        n1[m] = (normed * g1_ref[...] + s1_ref[...]).astype(BF16)
        for c in range(3):
            part = slice(c * inner, (c + 1) * inner)
            mix[m, :, part] = (
                dot(n1[m], wqkv_ref[:, part], 1, 0) + bmix_ref[:, part]
            ).astype(BF16)
        query_at = lax.broadcasted_iota(jnp.int32, (all_rows, all_rows), 0)
        key_at = lax.broadcasted_iota(jnp.int32, (all_rows, all_rows), 1)
        allowed = (segc == segr) & (key_at <= query_at)
        for h in range(heads):
            cols = slice(h * head_size, (h + 1) * head_size)
            q = mix[m, :, h * head_size : (h + 1) * head_size]
            k = mix[m, :, inner + h * head_size : inner + (h + 1) * head_size]
            v = mix[m, :, 2 * inner + h * head_size : 2 * inner + (h + 1) * head_size]
            scores = jnp.where(allowed, dot(q, k, 1, 1) * scale, MASKED)
            exps = jnp.exp(scores - jnp.max(scores, axis=-1, keepdims=True))
            p = exps / jnp.sum(exps, axis=-1, keepdims=True)
            probs[m, h] = p
            att[m, :, cols] = dot(p.astype(BF16), v, 1, 0).astype(BF16)
        for c in range(CHUNKS):
            send_part(m, 0, c, dot(att[m], wproj_ref[:, c * width : (c + 1) * width], 1, 0))
        after = rows + total_of(m, 0) + bproj_ref[...]
        aft[m] = after
        normed, unused = norm_parts(after)
        n2[m] = (normed * g2_ref[...] + s2_ref[...]).astype(BF16)
        for c in range(CHUNKS):
            part = slice(c * hwidth, (c + 1) * hwidth)
            x = dot(n2[m], wfc_ref[:, part], 1, 0) + bfc_ref[:, part]
            th = jnp.tanh(GELU_A * (x + GELU_B * (x * x * x)))
            act[m, :, part] = (0.5 * x * (1.0 + th)).astype(BF16)
            dgl[m, :, part] = 0.5 * (1.0 + th) + 0.5 * x * (1.0 - th * th) * (
                GELU_A * (1.0 + 3.0 * GELU_B * (x * x))
            )
        for c in range(CHUNKS):
            send_part(m, 1, c, dot(act[m], wout_ref[:, c * width : (c + 1) * width], 1, 0))
        valid = (segc < 2).astype(F32)
        result = valid * (aft[m] + total_of(m, 1) + bout_ref[...])
        outb[m] = result.astype(BF16).reshape(outb.shape[1:])

        @pl.when(section == 0)
        def _():
            pipe_copy(outb, xin, m, 0).start()

        prod_ref[m] = outb[m, portion]
        return carry

    lax.fori_loop(0, batches, forward, 0)

    def backward(m, carry):
        @pl.when(section == 0)
        def _():
            pipe_copy(inb, gin, m, 1).wait_recv()

        valid = (segc_ref[m] < 2).astype(F32)
        dy = valid * gin[m].reshape(all_rows, features).astype(F32)
        dyb[m] = dy.astype(BF16)
        for c in range(CHUNKS):
            part = slice(c * hwidth, (c + 1) * hwidth)
            d_pre = (dot(dyb[m], wout_ref[part, :], 1, 1) * dgl[m, :, part]).astype(BF16)
            dpre[m, :, part] = d_pre
        for c in range(CHUNKS):
            send_part(m, 2, c, dot(dpre[m], wfc_ref[c * width : (c + 1) * width, :], 1, 1))
        bias_fc = row_sum(dpre[m].astype(F32))
        for c in range(hidden // features):
            vec_ref[6 + c : 7 + c, :] += bias_fc[:, c * features : (c + 1) * features]
        vec_ref[5:6, :] += row_sum(dy)
        normed, inv_std = norm_parts(aft[m])
        d_norm = total_of(m, 2)
        vec_ref[3:4, :] += row_sum(d_norm * normed)
        vec_ref[4:5, :] += row_sum(d_norm)
        d_after = dy + norm_back(d_norm, normed, inv_std, g2_ref[...])
        aft[m] = d_after
        vec_ref[2:3, :] += row_sum(d_after)
        dab[m] = d_after.astype(BF16)
        dat[...] = dot(dab[m], wproj_ref[...], 1, 1).astype(BF16)
        for h in range(heads):
            at_q = slice(h * head_size, (h + 1) * head_size)
            at_k = slice(inner + h * head_size, inner + (h + 1) * head_size)
            at_v = slice(2 * inner + h * head_size, 2 * inner + (h + 1) * head_size)
            q, k, v = mix[m, :, at_q], mix[m, :, at_k], mix[m, :, at_v]
            d_att = dat[:, at_q]
            p = probs[m, h]
            dmix[m, :, at_v] = dot(p.astype(BF16), d_att, 0, 0).astype(BF16)
            d_p = dot(d_att, v, 1, 1)
            d_s = (p * (d_p - jnp.sum(d_p * p, axis=-1, keepdims=True))).astype(BF16)
            dmix[m, :, at_q] = (dot(d_s, k, 1, 0) * scale).astype(BF16)
            dmix[m, :, at_k] = (dot(d_s, q, 0, 0) * scale).astype(BF16)
        for c in range(CHUNKS):
            send_part(m, 3, c, dot(dmix[m], wqkv_ref[c * width : (c + 1) * width, :], 1, 1))
        vec_ref[8:9, 0:inner] += row_sum(dmix[m, :, 0:inner].astype(F32))
        vec_ref[8:9, inner : 2 * inner] += row_sum(dmix[m, :, 2 * inner :].astype(F32))
        normed, inv_std = norm_parts(xin[m].reshape(all_rows, features).astype(F32))
        d_norm = total_of(m, 3)
        vec_ref[0:1, :] += row_sum(d_norm * normed)
        vec_ref[1:2, :] += row_sum(d_norm)
        d_in = aft[m] + norm_back(d_norm, normed, inv_std, g1_ref[...])
        inb[m] = d_in.astype(BF16).reshape(inb.shape[1:])

        @pl.when(section == 1)
        def _():
            pipe_copy(inb, gin, m, 1).start()

        hand_ref[m] = inb[m, portion]
        return carry

    lax.fori_loop(0, batches, backward, 0)

    flat = batches * all_rows
    start = 0
    for left, right in ((n1, dmix), (n2, dpre), (dyb, act), (dab, att)):
        size = right.shape[-1]
        for c in range(CHUNKS):
            rows = slice(c * width, (c + 1) * width)
            grad_ref[rows, start : start + size] = dot(
                left[:, :, rows].reshape(flat, width), right[...].reshape(flat, size), 0, 0
            ).astype(BF16)
        start += size

    for m in range(batches):

        @pl.when(section == 0)
        def _():
            pipe_copy(outb, xin, m, 0).wait_send()

        @pl.when(section == 1)
        def _():
            pipe_copy(inb, gin, m, 1).wait_send()


def segment_ids(length_pair, all_rows, tile_rows):
    start_two = (length_pair[0] + tile_rows - 1) // tile_rows * tile_rows
    position = jnp.arange(all_rows, dtype=jnp.int32)
    inside_two = (position >= start_two) & (position < start_two + length_pair[1])
    return jnp.where(position < length_pair[0], 0, jnp.where(inside_two, 1, position + 2))


def local(
    block_input, cotangent, lengths, ln1_gain, ln1_bias, qkv_weight, qv_bias, proj_weight,
    proj_bias, ln2_gain, ln2_bias, fc_weight, fc_bias, out_weight, out_bias,
):
    groups = lax.axis_size("dp")
    tensors = lax.axis_size("tensor")
    batches, half_rows, features = block_input.shape[1:]
    all_rows = half_rows * tensors
    heads, head_size = qv_bias.shape[2:]
    inner = heads * head_size
    hidden = fc_weight.shape[2]
    segments = jax.vmap(lambda pair: segment_ids(pair, all_rows, all_rows // 2))(lengths[0])
    bmix = jnp.concatenate(
        [
            qv_bias[0, 0].reshape(1, inner),
            jnp.zeros((1, inner), F32),
            qv_bias[0, 1].reshape(1, inner),
        ],
        axis=1,
    )
    columns = 4 * inner + 2 * hidden
    vmem = pl.BlockSpec(memory_space=pltpu.VMEM)
    rows_of = lambda size, kind=BF16: pltpu.VMEM((batches, all_rows, size), kind)
    halves = pltpu.VMEM((batches, tensors, half_rows, features), BF16)
    swaps = pltpu.VMEM((batches, 4, CHUNKS, all_rows, features // CHUNKS), BF16)
    produced, handed, grads, vectors = pl.pallas_call(
        functools.partial(sections_kernel, heads, head_size),
        out_shape=(
            jax.ShapeDtypeStruct((batches, half_rows, features), BF16),
            jax.ShapeDtypeStruct((batches, half_rows, features), BF16),
            jax.ShapeDtypeStruct((features, columns), BF16),
            jax.ShapeDtypeStruct((16, features), F32),
        ),
        in_specs=[vmem] * 16,
        out_specs=(vmem,) * 4,
        scratch_shapes=[
            halves, halves, halves, halves,
            rows_of(features), rows_of(3 * inner),
            pltpu.VMEM((batches, heads, all_rows, all_rows), F32),
            rows_of(inner), rows_of(features, F32), rows_of(features), rows_of(hidden),
            rows_of(hidden, F32), rows_of(features), rows_of(hidden), rows_of(features),
            rows_of(3 * inner), pltpu.VMEM((all_rows, inner), BF16),
            swaps, swaps,
            pltpu.SemaphoreType.DMA((batches, 4, CHUNKS)),
            pltpu.SemaphoreType.DMA((batches, 4, CHUNKS)),
            pltpu.SemaphoreType.DMA, pltpu.SemaphoreType.DMA,
            pltpu.SemaphoreType.DMA((batches,)), pltpu.SemaphoreType.DMA((batches,)),
        ],
        compiler_params=pltpu.CompilerParams(
            collective_id=0, has_side_effects=True, vmem_limit_bytes=60 * 1024 * 1024
        ),
    )(
        block_input[0], cotangent[0], segments[:, :, None], segments[:, None, :],
        ln1_gain, ln1_bias, qkv_weight[0].reshape(features, 3 * inner), bmix, proj_weight[0],
        proj_bias, ln2_gain, ln2_bias, fc_weight[0], fc_bias[0].reshape(1, hidden),
        out_weight[0], out_bias,
    )
    block = features // groups
    received = lax.all_to_all(
        grads.reshape(groups, block, columns), "dp", split_axis=0, concat_axis=0, tiled=True
    )
    summed = jnp.sum(received.astype(F32), axis=0)
    g_qkv_w = summed[:, : 3 * inner].reshape(block, 3, inner)
    g_fc_w = summed[:, 3 * inner : 3 * inner + hidden]
    g_out_w = summed[:, 3 * inner + hidden : 3 * inner + 2 * hidden].T
    g_proj_w = summed[:, 3 * inner + 2 * hidden :].T
    vectors = lax.psum(vectors, "dp")
    group = lax.axis_index("dp")
    small = block // tensors
    own = lax.dynamic_slice_in_dim(
        vectors[:6], (group * tensors + lax.axis_index("tensor")) * small, small, 1
    )
    g_fc_b = lax.dynamic_slice_in_dim(vectors[6 : 6 + hidden // features], group * block, block, 1)
    cut = head_size // groups
    g_qv_b = lax.dynamic_slice_in_dim(
        vectors[8, : 2 * inner].reshape(2, heads, head_size), group * cut, cut, 2
    )
    return (
        produced[None, None],
        handed[None, None],
        own[0:1],
        own[1:2],
        g_qkv_w[None],
        g_qv_b[None],
        g_proj_w[None],
        own[2:3],
        own[3:4],
        own[4:5],
        g_fc_w[None],
        g_fc_b[None],
        g_out_w[None],
        own[5:6],
    )


def solution(mesh):
    return jax.shard_map(
        local,
        mesh=mesh,
        in_specs=(
            P("dp", None, "tensor", None),
            P("dp", None, "tensor", None),
            P("dp", None, None),
            P("pipe", None),
            P("pipe", None),
            P("pipe", None, None, "tensor"),
            P("pipe", None, "tensor", None),
            P("pipe", "tensor", None),
            P("pipe", None),
            P("pipe", None),
            P("pipe", None),
            P("pipe", None, "tensor"),
            P("pipe", "tensor", None),
            P("pipe", "tensor", None),
            P("pipe", None),
        ),
        out_specs=(
            P("pipe", "dp", None, "tensor", None),
            P("pipe", "dp", None, "tensor", None),
            P("pipe", ("dp", "tensor")),
            P("pipe", ("dp", "tensor")),
            P("pipe", "dp", None, "tensor"),
            P("pipe", None, "tensor", "dp"),
            P("pipe", "tensor", "dp"),
            P("pipe", ("dp", "tensor")),
            P("pipe", ("dp", "tensor")),
            P("pipe", ("dp", "tensor")),
            P("pipe", "dp", "tensor"),
            P("pipe", "tensor", "dp"),
            P("pipe", "tensor", "dp"),
            P("pipe", ("dp", "tensor")),
        ),
        check_vma=False,
    )
```

time: 935 us -> 332 us (0.36); the launches traced: 923 us -> 331 us
  local copies, waits for them, and re-layouts: 214 us -> 12.7 us
  other arithmetic: 201 us -> 7.27 us
  Pallas kernels: 0 us -> 147 us
  blocking collectives: 295 us -> 158 us
  waiting for transfers between devices: 103 us -> 0.01 us
  matrix products: 69.4 us -> 0 us
  between operations: 16.8 us -> 0.76 us
  starting transfers between devices: 17.1 us -> 5.94 us
    unnamed x1 -> x0, blocking collectives: 209 us -> none
    psum x0 -> x1, blocking collectives: none -> 158 us  [local(): vectors = lax.psum(vectors, 'dp')]
    pallas_call x0 -> x1, Pallas kernels: none -> 147 us  [local(): pl.pallas_call(functools.partial(sections_kernel, heads, head_size), out_...]
    reduce_scatter x12 -> x0, waiting for transfers between devices: 97.6 us -> none  [the longest x3 36.7 us: backward_step(): lax.psum_scatter(partial_one.astype(jnp.bfloat16), 'tensor', scatter_dime...]
    all_gather x12 -> x0, blocking collectives: 86.3 us -> none  [the longest x3 23.9 us: backward_step(): lax.all_gather(grad_mlp.astype(bf16), 'tensor', axis=0, tiled=True)]
    dot_general x38 -> x0, matrix products: 69.4 us -> none  [the longest x2 8.95 us: mlp_backward(): jnp.einsum('rd,fd->rf', gathered_grad, w_out, preferred_element_type=f32)]
    unnamed x65 -> x13, local copies, waits for them, and re-layouts: 69.7 us -> 5.52 us
    add x35 -> x0, other arithmetic: 52.4 us -> none  [the longest x12 45 us: backward_step(): totals = tuple((total + term for total, term in zip(totals, tick_grads)))]
  transfers between devices with their start and end apart: 19 -> 1, of which waited for: 11 -> 0; matrix products, arithmetic and copies ran while one was open for 15% -> 1% of each run, Pallas kernels for 0% -> 0%
where the time goes in v1:
time: 332 us; the launch traced here: 331 us
  blocking collectives  158 us (48%)
  Pallas kernels  147 us (44%)
  local copies, waits for them, and re-layouts  12.7 us (4%)
  other arithmetic  7.27 us (2%)
  starting transfers between devices  5.94 us (2%)
    psum x1, blocking collectives, local(): vectors = lax.psum(vectors, 'dp')  158 us
    pallas_call x1, Pallas kernels, local(): pl.pallas_call(functools.partial(sections_kernel, heads, head_size), out_...  147 us
  transfers between devices with their start and end apart: 1, of which 0 were waited for; matrix products, arithmetic and copies ran while one was open for 1% of the time, Pallas kernels for 0%

profile of v1, /device:TPU:0, one launch (start us, length us, event | category | flops | bytes accessed | tf_op | source)
XLA Modules:
  0.0 331.1 jit_solution(4084382651872369590)
XLA Ops:
  0.7 1.0 slice_reduce_fusion.3
  1.6 0.9 select_select_fusion.segc_ref
  2.5 0.7 compare_select_fusion.segr_ref
  3.1 0.8 slice_reduce_fusion.2
  3.9 0.1 reshape_squeeze.16
  4.0 0.1 reshape_squeeze.17
  4.1 2.6 copy.31
  6.7 2.3 copy.32.wqkv_ref
  9.0 0.6 copy.35
  9.6 0.6 fusion.1.bmix_ref
  10.2 146.6 %shard_map.254 = (bf16[2,128,768]{2,1,0:T(8,128)(2,1)}, bf16[2,128,768]{2,1,0:T(8,128)(2,1)}, bf16[768,4608]{1,0:T(8,128)(2,1)}, f32[16,768]{1,0:T(8,128)}) custom-call(bf16[2,128,768]{2,1,0:T(8,128)(2,1)} %bitcast.32, bf16[2,128,768]{2,1,0:T(8,128)(2,1)} %bitcast.33, s32[2,256,1]{2,1,0:T(8,128)} %select_select_fusion.segc_ref, ...), custom_call_target="tpu_custom_call" | custom-call | tf_op jit(solution)/shard_map/pallas_call | solution.py:298
  156.9 5.9 %all-to-all-start = ((bf16[8,96,4608]{2,1,0:T(8,128)(2,1)}), bf16[8,96,4608]{2,1,0:T(8,128)(2,1)}, u32[]{:S(2)}, u32[]{:S(2)}) async-start(bf16[8,96,4608]{2,1,0:T(8,128)(2,1)} %bitcast.27), calls=%async_computation | async-start | bytes 14155776 | tf_op jit(solution)/shard_map/all_to_all | solution.py:331
  162.8 157.8 %psum.7 = f32[16,768]{1,0:T(8,128)S(1)} all-reduce(f32[16,768]{1,0:T(8,128)S(1)} %copy-done.2), channel_id=1, replica_groups=mesh['pipe'=2,'dp'=8,'tensor'=2] {'dp'}, use_global_device_ids=true, to_apply=%region_0.1 | all-reduce | flops 12288 | bytes 98304 | tf_op jit(solution)/shard_map/psum | solution.py:339
  320.7 0.1 constant_dynamic-slice_fusion
  320.8 0.6 copy.37
  321.4 0.6 dynamic-slice_bitcast_fusion
  322.1 0.5 fusion.3
  322.7 4.2 %convert_reduce_fusion = f32[96,4608]{1,0:T(8,128)S(1)} fusion(bf16[8,96,4608]{2,1,0:T(8,128)(2,1)} %all-to-all-done), kind=kLoop, calls=%fused_computation | loop fusion | flops 6635520 | bytes 8847360 | tf_op jit(solution)/shard_map/reduce_sum | solution.py:334
  326.9 1.1 slice_bitcast_fusion
  328.0 0.7 slice_bitcast_fusion.2
  328.7 0.2 broadcast_in_dim_reshape.3
  328.8 0.8 copy.34
  329.6 0.7 copy.40
  330.4 0.7 copy.41
  (18 shorter events, 0.2 us)
Async XLA Ops:
  6.7 2.3 copy-start.3
  156.9 6.0 %copy-start.2 = (f32[16,768]{1,0:T(8,128)S(1)}, f32[16,768]{1,0:T(8,128)}, u32[]{:S(2)}) copy-start(f32[16,768]{1,0:T(8,128)} %get-tuple-element.20) | copy-start | bytes 147460
  156.9 165.8 %all-to-all-start = ((bf16[8,96,4608]{2,1,0:T(8,128)(2,1)}), bf16[8,96,4608]{2,1,0:T(8,128)(2,1)}, u32[]{:S(2)}, u32[]{:S(2)}) async-start(bf16[8,96,4608]{2,1,0:T(8,128)(2,1)} %bitcast.27), calls=%async_computation | async-start | bytes 14155776 | tf_op jit(solution)/shard_map/all_to_all | solution.py:331
  327.9 1.7 copy-start.1
  328.0 2.4 copy-start

commit v2 on v1

--- a/solution.py
+++ b/solution.py
@@ -43,12 +43,13 @@
 
 
 def sections_kernel(
-    heads, head_size,
+    heads, head_size, groups, direct,
     x_ref, g_ref, segc_ref, segr_ref, g1_ref, s1_ref, wqkv_ref, bmix_ref, wproj_ref, bproj_ref,
     g2_ref, s2_ref, wfc_ref, bfc_ref, wout_ref, bout_ref,
     prod_ref, hand_ref, grad_ref, vec_ref,
     xin, gin, outb, inb, n1, mix, probs, att, aft, n2, act, dgl, dyb, dpre, dab, dmix, dat,
     snd, rcv, send_sem, recv_sem, first_send, first_recv, pipe_send, pipe_recv,
+    gr, rx, rz, vx, vz, x_send, x_recv, z_send, z_recv, v_send, v_recv,
 ):
     section = lax.axis_index("pipe")
     portion = lax.axis_index("tensor")
@@ -62,7 +63,47 @@
     barrier = pltpu.get_barrier_semaphore()
     pl.semaphore_signal(barrier, inc=1, device_id={"tensor": 1 - portion}, device_id_type=MESH)
     pl.semaphore_signal(barrier, inc=1, device_id={"pipe": 1 - section}, device_id_type=MESH)
-    pl.semaphore_wait(barrier, 2)
+    layers = groups // 2
+    group = lax.axis_index("dp")
+    layer, side = group // 2, group % 2
+    across = {"dp": layer * 2 + 1 - side}
+    others = [{"dp": ((layer + step) % layers) * 2 + side} for step in range(1, layers)]
+    if direct:
+        for peer in [across] + others:
+            pl.semaphore_signal(barrier, inc=1, device_id=peer, device_id_type=MESH)
+        pl.semaphore_wait(barrier, 2 + layers)
+    else:
+        pl.semaphore_wait(barrier, 2)
+
+    def remote(source, target, sent, got, peer):
+        return pltpu.make_async_remote_copy(
+            src_ref=source, dst_ref=target, send_sem=sent, recv_sem=got,
+            device_id=peer, device_id_type=MESH,
+        )
+
+    def across_copy(j):
+        return remote(gr.at[j, :, 1 - side], rx.at[j], x_send.at[j], x_recv.at[j], across)
+
+    def layer_copy(j, step):
+        return remote(
+            gr.at[j, (layer + step) % layers, side], rz.at[j, step - 1],
+            z_send.at[j, step - 1], z_recv.at[j, step - 1], others[step - 1],
+        )
+
+    def weight_grad(first, left, right, cols):
+        flat = n1.shape[0] * n1.shape[1]
+        values = dot(
+            left[...].reshape(flat, left.shape[-1]),
+            right[:, :, cols].reshape(flat, cols.stop - cols.start), 0, 0,
+        ).astype(BF16)
+        for number in range(values.shape[1] // inner):
+            part = values[:, number * inner : (number + 1) * inner]
+            j = first + number
+            if direct:
+                gr[j] = part.reshape(gr.shape[1:])
+                across_copy(j).start()
+            else:
+                grad_ref[j] = part
 
     def first_copy(source, target):
         return pltpu.make_async_remote_copy(
@@ -196,6 +237,17 @@
             dpre[m, :, part] = d_pre
         for c in range(CHUNKS):
             send_part(m, 2, c, dot(dpre[m], wfc_ref[c * width : (c + 1) * width, :], 1, 1))
+        per = hidden // inner
+
+        @pl.when(m == batches - 1)
+        def _():
+            for c in range(2):
+                weight_grad(c * (per // 2), dyb, act, slice(c * hidden // 2, (c + 1) * hidden // 2))
+            for c in range(2):
+                weight_grad(
+                    per + c * (per // 2), n2, dpre, slice(c * hidden // 2, (c + 1) * hidden // 2)
+                )
+
         bias_fc = row_sum(dpre[m].astype(F32))
         for c in range(hidden // features):
             vec_ref[6 + c : 7 + c, :] += bias_fc[:, c * features : (c + 1) * features]
@@ -223,6 +275,12 @@
             dmix[m, :, at_k] = (dot(d_s, q, 0, 0) * scale).astype(BF16)
         for c in range(CHUNKS):
             send_part(m, 3, c, dot(dmix[m], wqkv_ref[c * width : (c + 1) * width, :], 1, 1))
+
+        @pl.when(m == batches - 1)
+        def _():
+            weight_grad(2 * per, dab, att, slice(0, inner))
+            weight_grad(2 * per + 1, n1, dmix, slice(0, 3 * inner))
+
         vec_ref[8:9, 0:inner] += row_sum(dmix[m, :, 0:inner].astype(F32))
         vec_ref[8:9, inner : 2 * inner] += row_sum(dmix[m, :, 2 * inner :].astype(F32))
         normed, inv_std = norm_parts(xin[m].reshape(all_rows, features).astype(F32))
@@ -241,16 +299,42 @@
 
     lax.fori_loop(0, batches, backward, 0)
 
-    flat = batches * all_rows
-    start = 0
-    for left, right in ((n1, dmix), (n2, dpre), (dyb, act), (dab, att)):
-        size = right.shape[-1]
-        for c in range(CHUNKS):
-            rows = slice(c * width, (c + 1) * width)
-            grad_ref[rows, start : start + size] = dot(
-                left[:, :, rows].reshape(flat, width), right[...].reshape(flat, size), 0, 0
-            ).astype(BF16)
-        start += size
+    if direct:
+        chunks = gr.shape[0]
+        vec_across = remote(vec_ref, vx, v_send.at[0], v_recv.at[0], across)
+        vec_across.start()
+
+        def relay(j, carry):
+            across_copy(j).wait()
+            gr[j, :, side] = (gr[j, :, side].astype(F32) + rx[j].astype(F32)).astype(BF16)
+            for step in range(1, layers):
+                layer_copy(j, step).start()
+            return carry
+
+        lax.fori_loop(0, chunks, relay, 0)
+        vec_across.wait()
+        vx[...] += vec_ref[...]
+        vec_copies = [
+            remote(vx, vz.at[step - 1], v_send.at[step], v_recv.at[step], others[step - 1])
+            for step in range(1, layers)
+        ]
+        for copy in vec_copies:
+            copy.start()
+
+        def finish(j, carry):
+            total = gr[j, layer, side].astype(F32)
+            for step in range(1, layers):
+                layer_copy(j, step).wait()
+                total = total + rz[j, step - 1].astype(F32)
+            grad_ref[j] = total
+            return carry
+
+        lax.fori_loop(0, chunks, finish, 0)
+        total = vx[...]
+        for step in range(1, layers):
+            vec_copies[step - 1].wait()
+            total = total + vz[step - 1]
+        vec_ref[...] = total
 
     for m in range(batches):
 
@@ -290,17 +374,28 @@
         ],
         axis=1,
     )
-    columns = 4 * inner + 2 * hidden
+    block = features // groups
+    direct = groups % 2 == 0 and block % 16 == 0
+    layers = groups // 2
+    per = hidden // inner
+    chunks = 4 + 2 * per
+    if direct:
+        grad_shape = jax.ShapeDtypeStruct((chunks, block, inner), F32)
+        slabs, hops = (chunks, layers, 2, block, inner), max(layers - 1, 1)
+    else:
+        grad_shape = jax.ShapeDtypeStruct((chunks, features, inner), BF16)
+        slabs, hops = (1, 1, 2, 16, 128), 1
+    dma = pltpu.SemaphoreType.DMA
     vmem = pl.BlockSpec(memory_space=pltpu.VMEM)
     rows_of = lambda size, kind=BF16: pltpu.VMEM((batches, all_rows, size), kind)
     halves = pltpu.VMEM((batches, tensors, half_rows, features), BF16)
     swaps = pltpu.VMEM((batches, 4, CHUNKS, all_rows, features // CHUNKS), BF16)
     produced, handed, grads, vectors = pl.pallas_call(
-        functools.partial(sections_kernel, heads, head_size),
+        functools.partial(sections_kernel, heads, head_size, groups, direct),
         out_shape=(
             jax.ShapeDtypeStruct((batches, half_rows, features), BF16),
             jax.ShapeDtypeStruct((batches, half_rows, features), BF16),
-            jax.ShapeDtypeStruct((features, columns), BF16),
+            grad_shape,
             jax.ShapeDtypeStruct((16, features), F32),
         ),
         in_specs=[vmem] * 16,
@@ -317,6 +412,11 @@
             pltpu.SemaphoreType.DMA((batches, 4, CHUNKS)),
             pltpu.SemaphoreType.DMA, pltpu.SemaphoreType.DMA,
             pltpu.SemaphoreType.DMA((batches,)), pltpu.SemaphoreType.DMA((batches,)),
+            pltpu.VMEM(slabs, BF16), pltpu.VMEM(slabs[:2] + slabs[3:], BF16),
+            pltpu.VMEM((slabs[0], hops) + slabs[3:], BF16),
+            pltpu.VMEM((16, features), F32), pltpu.VMEM((hops, 16, features), F32),
+            dma((slabs[0],)), dma((slabs[0],)), dma((slabs[0], hops)), dma((slabs[0], hops)),
+            dma((hops + 1,)), dma((hops + 1,)),
         ],
         compiler_params=pltpu.CompilerParams(
             collective_id=0, has_side_effects=True, vmem_limit_bytes=60 * 1024 * 1024
@@ -327,16 +427,17 @@
         proj_bias, ln2_gain, ln2_bias, fc_weight[0], fc_bias[0].reshape(1, hidden),
         out_weight[0], out_bias,
     )
-    block = features // groups
-    received = lax.all_to_all(
-        grads.reshape(groups, block, columns), "dp", split_axis=0, concat_axis=0, tiled=True
-    )
-    summed = jnp.sum(received.astype(F32), axis=0)
-    g_qkv_w = summed[:, : 3 * inner].reshape(block, 3, inner)
-    g_fc_w = summed[:, 3 * inner : 3 * inner + hidden]
-    g_out_w = summed[:, 3 * inner + hidden : 3 * inner + 2 * hidden].T
-    g_proj_w = summed[:, 3 * inner + 2 * hidden :].T
-    vectors = lax.psum(vectors, "dp")
+    if not direct:
+        received = lax.all_to_all(
+            grads.reshape(chunks, groups, block, inner).swapaxes(0, 1), "dp",
+            split_axis=0, concat_axis=0, tiled=True,
+        )
+        grads = jnp.sum(received.astype(F32), axis=0)
+        vectors = lax.psum(vectors, "dp")
+    g_out_w = grads[:per].transpose(0, 2, 1).reshape(hidden, block)
+    g_fc_w = grads[per : 2 * per].transpose(1, 0, 2).reshape(block, hidden)
+    g_proj_w = grads[2 * per].T
+    g_qkv_w = grads[2 * per + 1 :].transpose(1, 0, 2)
     group = lax.axis_index("dp")
     small = block // tensors
     own = lax.dynamic_slice_in_dim(

time: 332 us -> 228 us (0.69)
  blocking collectives: 158 us -> 0 us
  Pallas kernels: 147 us -> 204 us
  local copies, waits for them, and re-layouts: 12.7 us -> 19.7 us
  starting transfers between devices: 5.94 us -> 0 us
  other arithmetic: 7.27 us -> 3.08 us
    psum x1 -> x0, blocking collectives: 158 us -> none  [local(): vectors = lax.psum(vectors, 'dp')]
    pallas_call x1, Pallas kernels: 147 us -> 204 us  [local(): pl.pallas_call(functools.partial(sections_kernel, heads, head_size, group...]
    all_to_all x1 -> x0, starting transfers between devices: 5.94 us -> none  [local(): lax.all_to_all(grads.reshape(groups, block, columns), 'dp', split_axis=0,...]
    reduce_sum x1 -> x0, other arithmetic: 4.19 us -> none  [local(): summed = jnp.sum(received.astype(F32), axis=0)]
  transfers between devices with their start and end apart: 1 -> 0, of which waited for: 0 -> 0; matrix products, arithmetic and copies ran while one was open for 1% -> 0% of each run, Pallas kernels for 0% -> 0%
where the time goes in v2:
time: 228 us
  Pallas kernels  204 us (89%)
  local copies, waits for them, and re-layouts  19.7 us (9%)
  other arithmetic  3.08 us (1%)
    pallas_call x1, Pallas kernels, local(): pl.pallas_call(functools.partial(sections_kernel, heads, head_size, group...  204 us
    unnamed x10, local copies, waits for them, and re-layouts  4.73 us

profile of v2, /device:TPU:0, one launch (start us, length us, event | category | flops | bytes accessed | tf_op | source)
XLA Modules:
  0.0 227.7 jit_solution(1876397332117774609)
XLA Ops:
  0.6 1.0 slice_reduce_fusion.3
  1.6 0.9 select_select_fusion.segc_ref
  2.5 0.7 compare_select_fusion.segr_ref
  3.1 0.8 slice_reduce_fusion.2
  4.1 0.6 fusion.1.bmix_ref
  4.7 2.6 %copy.31 = bf16[1,768,3,384]{1,3,2,0:T(8,128)(2,1)S(1)} copy(bf16[1,768,3,384]{3,1,2,0:T(8,128)(2,1)} %param.20) | data formatting | bytes 3538944 | tf_op args[5]
  7.3 2.2 copy.32.wqkv_ref
  9.6 0.6 copy.36
  10.2 204.2 %shard_map.254 = (bf16[2,128,768]{2,1,0:T(8,128)(2,1)}, bf16[2,128,768]{2,1,0:T(8,128)(2,1)}, f32[12,96,384]{2,1,0:T(8,128)}, f32[16,768]{1,0:T(8,128)}) custom-call(bf16[2,128,768]{2,1,0:T(8,128)(2,1)} %bitcast.36, bf16[2,128,768]{2,1,0:T(8,128)(2,1)} %bitcast.37, s32[2,256,1]{2,1,0:T(8,128)} %select_select_fusion.segc_ref, ...), custom_call_target="tpu_custom_call" | custom-call | tf_op jit(solution)/shard_map/pallas_call | solution.py:393
  214.4 0.7 slice.56
  215.2 0.5 fusion.3
  215.8 0.8 slice_reduce_fusion
  216.7 0.6 copy.38
  217.3 0.7 slice.66
  218.0 0.6 dynamic-slice_bitcast_fusion
  218.6 1.3 slice_bitcast_fusion
  220.0 0.4 copy.34
  220.4 1.1 broadcast_in_dim_reshape.6
  221.4 0.4 copy.35
  221.8 1.1 broadcast_in_dim_reshape.7
  222.9 1.8 slice_bitcast_fusion.2
  224.7 1.6 slice_bitcast_fusion.3
  226.3 0.7 copy.41
  227.0 0.7 copy.42
  (14 shorter events, 0.4 us)
Async XLA Ops:
  7.3 2.3 copy-start.2
  221.4 4.8 %copy-start.1 = (bf16[2,128,768]{2,1,0:T(8,128)(2,1)S(1)}, bf16[2,128,768]{2,1,0:T(8,128)(2,1)}, u32[]{:S(2)}) copy-start(bf16[2,128,768]{2,1,0:T(8,128)(2,1)} %get-tuple-element.18) | copy-start | bytes 1179652
  221.8 5.2 %copy-start = (bf16[2,128,768]{2,1,0:T(8,128)(2,1)S(1)}, bf16[2,128,768]{2,1,0:T(8,128)(2,1)}, u32[]{:S(2)}) copy-start(bf16[2,128,768]{2,1,0:T(8,128)(2,1)} %get-tuple-element.19) | copy-start | bytes 1179652

commit v3 on v2

--- a/solution.py
+++ b/solution.py
@@ -89,6 +89,13 @@
             gr.at[j, (layer + step) % layers, side], rz.at[j, step - 1],
             z_send.at[j, step - 1], z_recv.at[j, step - 1], others[step - 1],
         )
+
+    def relay(j, carry):
+        across_copy(j).wait()
+        gr[j, :, side] = (gr[j, :, side].astype(F32) + rx[j].astype(F32)).astype(BF16)
+        for step in range(1, layers):
+            layer_copy(j, step).start()
+        return carry
 
     def weight_grad(first, left, right, cols):
         flat = n1.shape[0] * n1.shape[1]
@@ -280,6 +287,8 @@
         def _():
             weight_grad(2 * per, dab, att, slice(0, inner))
             weight_grad(2 * per + 1, n1, dmix, slice(0, 3 * inner))
+            if direct:
+                lax.fori_loop(0, per, relay, 0)
 
         vec_ref[8:9, 0:inner] += row_sum(dmix[m, :, 0:inner].astype(F32))
         vec_ref[8:9, inner : 2 * inner] += row_sum(dmix[m, :, 2 * inner :].astype(F32))
@@ -304,14 +313,7 @@
         vec_across = remote(vec_ref, vx, v_send.at[0], v_recv.at[0], across)
         vec_across.start()
 
-        def relay(j, carry):
-            across_copy(j).wait()
-            gr[j, :, side] = (gr[j, :, side].astype(F32) + rx[j].astype(F32)).astype(BF16)
-            for step in range(1, layers):
-                layer_copy(j, step).start()
-            return carry
-
-        lax.fori_loop(0, chunks, relay, 0)
+        lax.fori_loop(hidden // inner, chunks, relay, 0)
         vec_across.wait()
         vx[...] += vec_ref[...]
         vec_copies = [

time: 228 us -> 223 us (0.978)
  Pallas kernels: 204 us -> 199 us
    pallas_call x1, Pallas kernels: 204 us -> 199 us  [local(): pl.pallas_call(functools.partial(sections_kernel, heads, head_size, group...]
where the time goes in v3:
time: 223 us; the launch traced here: 222 us
  Pallas kernels  199 us (89%)
  local copies, waits for them, and re-layouts  19.7 us (9%)
  other arithmetic  3.08 us (1%)
    pallas_call x1, Pallas kernels, local(): pl.pallas_call(functools.partial(sections_kernel, heads, head_size, group...  199 us
    unnamed x10, local copies, waits for them, and re-layouts  4.73 us

profile of v3, /device:TPU:0, one launch (start us, length us, event | category | flops | bytes accessed | tf_op | source)
XLA Modules:
  0.0 222.2 jit_solution(6436488585041670976)
XLA Ops:
  0.6 1.0 slice_reduce_fusion.3
  1.6 0.9 select_select_fusion.segc_ref
  2.5 0.7 compare_select_fusion.segr_ref
  3.1 0.8 slice_reduce_fusion.2
  4.1 0.6 fusion.1.bmix_ref
  4.7 2.6 %copy.31 = bf16[1,768,3,384]{1,3,2,0:T(8,128)(2,1)S(1)} copy(bf16[1,768,3,384]{3,1,2,0:T(8,128)(2,1)} %param.20) | data formatting | bytes 3538944 | tf_op args[5]
  7.3 2.2 %copy.32.wqkv_ref = bf16[768,1152]{1,0:T(8,128)(2,1)} copy(bf16[768,1152]{0,1:T(8,128)(2,1)S(1)} %bitcast.32) | data formatting | bytes 3538944 | tf_op jit(solution)/shard_map/reshape;squeeze | solution.py:428
  9.6 0.6 copy.36
  10.2 198.7 %shard_map.254 = (bf16[2,128,768]{2,1,0:T(8,128)(2,1)}, bf16[2,128,768]{2,1,0:T(8,128)(2,1)}, f32[12,96,384]{2,1,0:T(8,128)}, f32[16,768]{1,0:T(8,128)}) custom-call(bf16[2,128,768]{2,1,0:T(8,128)(2,1)} %bitcast.36, bf16[2,128,768]{2,1,0:T(8,128)(2,1)} %bitcast.37, s32[2,256,1]{2,1,0:T(8,128)} %select_select_fusion.segc_ref, ...), custom_call_target="tpu_custom_call" | custom-call | tf_op jit(solution)/shard_map/pallas_call | solution.py:395
  208.9 0.7 slice.56
  209.7 0.5 fusion.3
  210.2 0.8 slice_reduce_fusion
  211.1 0.6 copy.38
  211.7 0.7 slice.66
  212.5 0.6 dynamic-slice_bitcast_fusion
  213.1 1.3 slice_bitcast_fusion
  214.4 0.4 copy.34
  214.8 1.1 broadcast_in_dim_reshape.6
  215.9 0.4 copy.35
  216.3 1.1 broadcast_in_dim_reshape.7
  217.3 1.8 slice_bitcast_fusion.2
  219.1 1.6 slice_bitcast_fusion.3
  220.7 0.7 copy.41
  221.5 0.7 copy.42
  (14 shorter events, 0.4 us)
Async XLA Ops:
  7.3 2.3 %copy-start.2 = (f32[1,2,768]{2,1,0:T(2,128)S(1)}, f32[1,2,768]{2,1,0:T(2,128)}, u32[]{:S(2)}) copy-start(f32[1,2,768]{2,1,0:T(2,128)} %param.27) | copy-start | bytes 18436
  215.9 4.8 %copy-start.1 = (bf16[2,128,768]{2,1,0:T(8,128)(2,1)S(1)}, bf16[2,128,768]{2,1,0:T(8,128)(2,1)}, u32[]{:S(2)}) copy-start(bf16[2,128,768]{2,1,0:T(8,128)(2,1)} %get-tuple-element.18) | copy-start | bytes 1179652
  216.3 5.2 %copy-start = (bf16[2,128,768]{2,1,0:T(8,128)(2,1)S(1)}, bf16[2,128,768]{2,1,0:T(8,128)(2,1)}, u32[]{:S(2)}) copy-start(bf16[2,128,768]{2,1,0:T(8,128)(2,1)} %get-tuple-element.19) | copy-start | bytes 1179652
